TPU v7x, 32 devices: a whole 2x2x4 slice. The times are simulated.
32 devices in a mesh: seq: 8 (over z, x), tp: 4 (over y, core).
Axes of the slice: x: 2, y: 2, z: 4, core: 2. Of those that a mesh axis runs over, the one named last changes fastest.
Arguments:
- x_in: bfloat16 [6144, 1024], P('seq', 'tp'), may hold values from -6 to 6
- ln_gain: float32 [1024], replicated, may hold values from 0.1 to 1.9
- ln_bias: float32 [1024], replicated, may hold values from -4 to 4
- w_qkv: bfloat16 [3, 1024, 1024], P(None, None, 'tp'), may hold values from -0.25 to 0.25
- w_o: bfloat16 [1024, 1024], P('tp'), may hold values from -1 to 1
- w_in: bfloat16 [1024, 4096], P(None, 'tp'), may hold values from -0.1875 to 0.1875
- b_in: float32 [4096], P('tp'), may hold values from -4 to 4
- w_out: bfloat16 [4096, 1024], P('tp'), may hold values from -0.09375 to 0.09375
- b_out: float32 [1024], P('tp'), may hold values from -4 to 4
- grad_out: bfloat16 [6144, 1024], P('seq', 'tp'), may hold values from -6 to 6
- segment_ids: int32 [6144], P('seq'), may hold values from 0 to 215, as said below
- pad_mask: int32 [6144], P('seq'), may hold values from 0 to 1, as said below
Outputs:
- mixed: bfloat16 [6144, 1024], P('seq', 'tp')
- grad_input: float32 [6144, 1024], P('seq', 'tp')
- grad_gain: float32 [1024], P('tp')
- grad_bias: float32 [1024], P('tp')
- grad_qkv: float32 [3, 1024, 1024], P(None, None, 'tp')
- grad_wo: float32 [1024, 1024], P('tp')
- grad_win: float32 [1024, 4096], P(None, 'tp')
- grad_bin: float32 [4096], P('tp')
- grad_wout: float32 [4096, 1024], P('tp')
- grad_bout: float32 [1024], P('tp')
Inputs may be any that keep to these rules, and one draw needn't show every extreme that they name: `segment_ids`: ids never fall along the tokens; the tokens form packs of 1024 that no id crosses; a pack holds whole proteins of 30 to 1024 residues, each with an id of its own, followed by the pack's padding, which has one more id of its own; some pack holds a single protein of exactly 1024 residues; the last pack ends in padding. `pad_mask`: 0 exactly on the padding tokens of each pack.
All inputs are finite; a program needn't handle non-finite values.
Results may differ from a plain program's by a relative error of at most 0.012.
The roundings to bfloat16 on the way count: a program that leaves them out, or rounds other values in their place, can miss the bound.
Values may be sent and summed in bfloat16 or wider, within the bound.
A program may use at most 128 MiB of HBM per device.

v0:
```python
import jax
import jax.numpy as jnp
from jax import lax
from jax.sharding import PartitionSpec as P

PACK = 1024


LOG2E = 1.4426950408889634
EPSILON = 1e-05


def passed_along(value, axis, steps):
    count = lax.axis_size(axis)
    leading, last = (max(0, -steps), min(count, count - steps))
    return lax.ppermute(value, axis, [(source, source + steps) for source in range(leading, last)])


def angles(first_row, rows_count):
    places = ((first_row + jnp.arange(rows_count, dtype=jnp.int32)) % PACK).astype(jnp.float32)
    inverse = 10000.0 ** (-(jnp.arange(16, dtype=jnp.float32) * 2.0) / 32.0)
    phase = places[:, None] * inverse[None, :]
    return (jnp.cos(phase), jnp.sin(phase))


def rotate(source, cosine, sine, sense):
    rows_count, head_count = (source.shape[0], source.shape[1])
    paired = source[..., :32].reshape(rows_count, head_count, 16, 2)
    even_part = paired[..., 0]
    odd_part = paired[..., 1]
    cos_rows = cosine[:, None, :]
    sin_rows = sense * sine[:, None, :]
    turned = jnp.stack(
        [even_part * cos_rows - odd_part * sin_rows, odd_part * cos_rows + even_part * sin_rows], -1
    )
    return jnp.concatenate([turned.reshape(rows_count, head_count, 32), source[..., 32:]], -1)


def permitted(query_tags, query_first, key_tags, key_first, limit):
    query_place = query_first + jnp.arange(query_tags.shape[0], dtype=jnp.int32)
    key_place = key_first + jnp.arange(key_tags.shape[0], dtype=jnp.int32)
    causal = (
        (key_place[None, :] <= query_place[:, None])
        & (key_place[None, :] >= 0)
        & (query_place[:, None] < limit)
    )
    same_doc = key_tags[None, :] == query_tags[:, None]
    return causal & same_doc | (key_place[None, :] == query_place[:, None])


def base_two(query_rot, key_part):
    return (
        0.125
        * jnp.einsum("qhd,khd->hqk", query_rot, key_part, preferred_element_type=jnp.float32)
        * LOG2E
    )


def shards(
    x_in, ln_gain, ln_bias, w_qkv, w_o, w_in, b_in, w_out, b_out, grad_out, segment_ids, pad_mask
):
    rows_local = x_in.shape[0]
    width_local = x_in.shape[1]
    head_count = w_qkv.shape[2] // 64
    head_width = head_count * 64
    tp_rank = lax.axis_index("tp")
    row_first = lax.axis_index("seq") * rows_local
    limit = lax.axis_size("seq") * rows_local
    reach = (PACK - 2) // rows_local + 1
    key_tags = jnp.where(pad_mask == 1, segment_ids, -1)
    cosine, sine = angles(row_first, rows_local)
    whole = lax.all_gather(x_in, "tp", axis=1, tiled=True)
    inputs = whole.astype(jnp.float32)
    center = inputs - jnp.mean(inputs, -1, keepdims=True)
    inverse = lax.rsqrt(jnp.mean(center * center, -1, keepdims=True) + EPSILON)
    normed = center * inverse
    ln_out = (normed * ln_gain + ln_bias).astype(jnp.bfloat16)

    def project(which):
        return jnp.dot(ln_out, w_qkv[which], preferred_element_type=jnp.float32).reshape(
            rows_local, head_count, 64
        )

    query_rot = rotate(project(0), cosine, sine, 1.0).astype(jnp.bfloat16)
    key_rot = rotate(project(1), cosine, sine, 1.0).astype(jnp.bfloat16)
    values = project(2).astype(jnp.bfloat16)
    query_flat = query_rot.reshape(rows_local, head_width)
    key_flat = key_rot.reshape(rows_local, head_width)
    value_flat = values.reshape(rows_local, head_width)
    received = []
    for step in range(1, reach + 1):
        received.append(passed_along((key_flat, value_flat, key_tags), "seq", step))
    earliest = received[::-1]
    key_cat = jnp.concatenate([part[0] for part in earliest] + [key_flat], 0)
    value_cat = jnp.concatenate([part[1] for part in earliest] + [value_flat], 0)
    tag_cat = jnp.concatenate([part[2] for part in earliest] + [key_tags], 0)
    key_first = row_first - reach * rows_local
    key_heads = key_cat.reshape(-1, head_count, 64)
    value_heads = value_cat.reshape(-1, head_count, 64)
    mask_now = permitted(segment_ids, row_first, tag_cat, key_first, limit)[None]
    logit = base_two(query_rot, key_heads)
    ceiling = jnp.floor(jnp.max(jnp.where(mask_now, logit, -1e30), axis=2))
    weight = jnp.where(mask_now, jnp.exp2(logit - ceiling[:, :, None]), 0.0)
    totals = jnp.sum(weight, 2)
    accum = jnp.einsum(
        "hqk,khd->qhd", weight.astype(jnp.bfloat16), value_heads, preferred_element_type=jnp.float32
    )
    context = accum / totals.T[:, :, None]
    context_low = context.astype(jnp.bfloat16).reshape(rows_local, head_width)
    hidden_pre = jnp.dot(ln_out, w_in, preferred_element_type=jnp.float32) + b_in
    activ_low = jax.nn.gelu(hidden_pre, approximate=True).astype(jnp.bfloat16)
    branch = jnp.dot(context_low, w_o, preferred_element_type=jnp.float32) + jnp.dot(
        activ_low, w_out, preferred_element_type=jnp.float32
    )
    summed = lax.psum_scatter(branch, "tp", scatter_dimension=1, tiled=True)
    mixed = (x_in.astype(jnp.float32) + summed + b_out).astype(jnp.bfloat16)
    grad_whole = lax.all_gather(grad_out, "tp", axis=1, tiled=True)
    grad_wo = jnp.dot(context_low.T, grad_whole, preferred_element_type=jnp.float32)
    grad_wout = jnp.dot(activ_low.T, grad_whole, preferred_element_type=jnp.float32)
    grad_bout = jnp.sum(grad_out.astype(jnp.float32), 0)
    grad_context = jnp.dot(grad_whole, w_o.T, preferred_element_type=jnp.float32).reshape(
        rows_local, head_count, 64
    )
    grad_activ = jnp.dot(grad_whole, w_out.T, preferred_element_type=jnp.float32)
    gelu_pull = jax.vjp(lambda pre: jax.nn.gelu(pre, approximate=True), hidden_pre)[1]
    grad_hidden = gelu_pull(grad_activ)[0].astype(jnp.bfloat16)
    grad_win = jnp.dot(ln_out.T, grad_hidden, preferred_element_type=jnp.float32)
    grad_bin = jnp.sum(grad_hidden.astype(jnp.float32), 0)
    grad_accum = (grad_context / totals.T[:, :, None]).astype(jnp.bfloat16)
    offset_term = jnp.sum(grad_context * context, -1).T / totals
    grad_accum_flat = grad_accum.reshape(rows_local, head_width)

    def score_grads(
        query_part,
        grad_part,
        ceil_part,
        offs_part,
        query_tags,
        query_first,
        key_part,
        value_part,
        tag_part,
        part_first,
    ):
        mask_part = permitted(query_tags, query_first, tag_part, part_first, limit)[None]
        weight_part = jnp.where(
            mask_part, jnp.exp2(base_two(query_part, key_part) - ceil_part[:, :, None]), 0.0
        )
        grad_weight = (
            jnp.einsum("qhd,khd->hqk", grad_part, value_part, preferred_element_type=jnp.float32)
            - offs_part[:, :, None]
        )
        return (weight_part.astype(jnp.bfloat16), (weight_part * grad_weight).astype(jnp.bfloat16))

    weight_low, grad_logit = score_grads(
        query_rot,
        grad_accum,
        ceiling,
        offset_term,
        segment_ids,
        row_first,
        key_heads,
        value_heads,
        tag_cat,
        key_first,
    )
    grad_query_rot = 0.125 * jnp.einsum(
        "hqk,khd->qhd", grad_logit, key_heads, preferred_element_type=jnp.float32
    )
    arrived = [(query_flat, grad_accum_flat, ceiling.T, offset_term.T, segment_ids)]
    for step in range(1, reach + 1):
        arrived.append(
            (
                passed_along(query_flat.astype(jnp.float32), "seq", -step).astype(query_flat.dtype),
                passed_along(grad_accum_flat.astype(jnp.float32), "seq", -step).astype(
                    grad_accum_flat.dtype
                ),
                passed_along(ceiling.T, "seq", -step),
                passed_along(offset_term.T, "seq", -step),
                passed_along(segment_ids, "seq", -step),
            )
        )
    query_cat = jnp.concatenate([part[0] for part in arrived], 0)
    grad_cat = jnp.concatenate([part[1] for part in arrived], 0)
    ceil_cat = jnp.concatenate([part[2] for part in arrived], 0).T
    offs_cat = jnp.concatenate([part[3] for part in arrived], 0).T
    qtag_cat = jnp.concatenate([part[4] for part in arrived], 0)
    query_heads = query_cat.reshape(-1, head_count, 64)
    grad_heads = grad_cat.reshape(-1, head_count, 64)
    weight_back, logit_back = score_grads(
        query_heads,
        grad_heads,
        ceil_cat,
        offs_cat,
        qtag_cat,
        row_first,
        key_rot,
        values,
        key_tags,
        row_first,
    )
    grad_key_rot = 0.125 * jnp.einsum(
        "hqk,qhd->khd", logit_back, query_heads, preferred_element_type=jnp.float32
    )
    grad_value_sum = jnp.einsum(
        "hqk,qhd->khd", weight_back, grad_heads, preferred_element_type=jnp.float32
    )
    grad_query = (
        rotate(grad_query_rot, cosine, sine, -1.0)
        .astype(jnp.bfloat16)
        .reshape(rows_local, head_width)
    )
    grad_key = (
        rotate(grad_key_rot, cosine, sine, -1.0)
        .astype(jnp.bfloat16)
        .reshape(rows_local, head_width)
    )
    grad_values = grad_value_sum.astype(jnp.bfloat16).reshape(rows_local, head_width)
    grad_qkv = jnp.stack(
        [
            jnp.dot(ln_out.T, grad_query, preferred_element_type=jnp.float32),
            jnp.dot(ln_out.T, grad_key, preferred_element_type=jnp.float32),
            jnp.dot(ln_out.T, grad_values, preferred_element_type=jnp.float32),
        ]
    )
    grad_norm_part = (
        jnp.dot(grad_query, w_qkv[0].T, preferred_element_type=jnp.float32)
        + jnp.dot(grad_key, w_qkv[1].T, preferred_element_type=jnp.float32)
        + jnp.dot(grad_values, w_qkv[2].T, preferred_element_type=jnp.float32)
        + jnp.dot(grad_hidden, w_in.T, preferred_element_type=jnp.float32)
    )
    feature_first = tp_rank * width_local
    grad_norm = lax.psum(grad_norm_part, "tp")
    grad_gain = lax.dynamic_slice_in_dim(
        jnp.sum(grad_norm * normed, 0), feature_first, width_local, 0
    )
    grad_bias = lax.dynamic_slice_in_dim(jnp.sum(grad_norm, 0), feature_first, width_local, 0)
    grad_hat = grad_norm * ln_gain
    row_mean = jnp.mean(grad_hat, -1, keepdims=True)
    row_cross = jnp.mean(grad_hat * normed, -1, keepdims=True)
    grad_full = inverse * (grad_hat - row_mean - normed * row_cross)
    grad_input = lax.dynamic_slice_in_dim(
        grad_full, feature_first, width_local, 1
    ) + grad_out.astype(jnp.float32)
    totals_out = lax.psum(
        (grad_qkv, grad_wo, grad_win, grad_bin, grad_wout, grad_bout, grad_gain, grad_bias), "seq"
    )
    return (
        mixed,
        grad_input,
        totals_out[6],
        totals_out[7],
        totals_out[0],
        totals_out[1],
        totals_out[2],
        totals_out[3],
        totals_out[4],
        totals_out[5],
    )


def solution(mesh):
    return jax.shard_map(
        shards,
        mesh=mesh,
        in_specs=(
            P("seq", "tp"),
            P(),
            P(),
            P(None, None, "tp"),
            P("tp", None),
            P(None, "tp"),
            P("tp"),
            P("tp", None),
            P("tp"),
            P("seq", "tp"),
            P("seq"),
            P("seq"),
        ),
        out_specs=(
            P("seq", "tp"),
            P("seq", "tp"),
            P("tp"),
            P("tp"),
            P(None, None, "tp"),
            P("tp", None),
            P(None, "tp"),
            P("tp"),
            P("tp", None),
            P("tp"),
        ),
        check_vma=False,
    )
```

profile of v0, /device:TPU:0, one launch (start us, length us, event | category | flops | bytes accessed | tf_op | source)
XLA Modules:
  0.0 794.6 jit_solution(18122028457989374840)
XLA Ops:
  8.7 4.8 collective-permute-start.3
  13.5 3.5 collective-permute-start.2
  27.1 4.2 compare_or_fusion.1
  31.3 4.4 compare_or_fusion
  49.3 5.3 collective-permute-start.5
  54.6 4.6 collective-permute-start.4
  60.2 2.9 fusion.38
  63.1 5.2 collective-permute-start.1
  71.2 13.0 %collective-permute-start.7 = (bf16[768,256]{0,1:T(8,128)(2,1)S(1)}, bf16[768,256]{0,1:T(8,128)(2,1)}, u32[]{:S(2)}, u32[]{:S(2)}) collective-permute-start(bf16[768,256]{0,1:T(8,128)(2,1)S(1)} %bitcast.130), channel_id=1, source_target_pairs={{8,0},{12,4},{16,8},{20,12},{24,16},{28,20},{9,1},{13,5},{17,9},{2... | collective-permute-start | bytes 1179656 | tf_op jit(solution)/shard_map/ppermute | solution.py:16
  84.3 5.5 fusion.94
  89.8 5.9 convert_reduce_fusion.1
  95.8 3.5 fusion.95
  100.6 13.7 %select_reduce_fusion = (f32[4,768]{1,0:T(4,128)S(1)}, f32[4,768,2304]{2,1,0:T(8,128)}) fusion(pred[768,2304]{1,0:T(8,128)(4,1)S(1)} %copy-done.5, bf16[768,4,64]{0,2,1:T(8,128)(2,1)} %maximum_convert_fusion.1, bf16[768,4,64]{0,2,1:T(8,128)(2,1)} %bitcast.15, bf16[768,4,64]{0,2,1:T(8,128)(2,1)} %bitcast.14, bf16[768,4,32]{0,2,1:T(8,128)(2,1)S(1)} %slice.82, ...), kind=kOutput, calls=%fused_computation.4 | convolution fusion | flops 931525632 | bytes 31666176 | tf_op jit(solution)/shard_map/qhd,khd->hqk/dot_general | solution.py:54
  114.4 15.0 %fusion.12 = f32[4,768]{1,0:T(4,128)S(1)} fusion(f32[4,768]{1,0:T(4,128)S(1)} %get-tuple-element.49, f32[4,768,2304]{2,1,0:T(8,128)} %get-tuple-element.54, pred[768,2304]{1,0:T(8,128)(4,1)S(1)} %copy-done.5), kind=kLoop, calls=%fused_computation.15 | loop fusion | flops 35386368 | bytes 30105600 | tf_op jit(solution)/shard_map/reduce_sum | solution.py:104
  131.1 14.3 %multiply_reduce_fusion.2 = (f32[768,4]{0,1:T(4,128)S(1)}, bf16[768,4,64]{0,2,1:T(8,128)(2,1)}) fusion(f32[768,256]{0,1:T(8,128)} %get-tuple-element.57, f32[768,4]{0,1:T(4,128)S(1)} %bitcast.141, f32[4,768]{1,0:T(4,128)S(1)} %get-tuple-element.49, f32[4,768,2304]{2,1,0:T(8,128)} %get-tuple-element.54, pred[768,2304]{1,0:T(8,128)(4,1)} %compare_or_fusion.1, ...), kind=kOutput, calls=%fused_computation.75 | convolution fusion | flops 945681408 | bytes 32477184 | tf_op jit(solution)/shard_map/hqk,khd->qhd/dot_general | solution.py:105
  149.9 17.9 %fusion.37 = f32[768,4,64]{0,2,1:T(8,128)} fusion(f32[4,768]{1,0:T(4,128)} %bitcast_divide_fusion.1, f32[4,768]{1,0:T(4,128)S(1)} %get-tuple-element.49, f32[4,768,2304]{2,1,0:T(8,128)} %get-tuple-element.54, pred[768,2304]{1,0:T(8,128)(4,1)} %compare_or_fusion.1, bf16[768,4,64]{0,2,1:T(8,128)(2,1)} %maximum_convert_fusion.1, ...), kind=kOutput, calls=%fused_computation.55 | convolution fusion | flops 1869152256 | bytes 34050048 | tf_op jit(solution)/shard_map/hqk,khd->qhd/dot_general | solution.py:167
  169.5 12.0 %fusion.55 = f32[4,2304,768]{2,1,0:T(8,128)} fusion(bf16[768,4,64]{0,2,1:T(8,128)(2,1)} %bitcast.26, bf16[768,4,64]{0,2,1:T(8,128)(2,1)} %bitcast.24, bf16[768,4,64]{0,2,1:T(8,128)(2,1)S(1)} %maximum_convert_fusion, bf16[768,4,32]{0,2,1:T(8,128)(2,1)S(1)} %slice.86, bf16[768,4,32]{0,2,1:T(8,128)(2,1)S(1)} %reshape.490), kind=kOutput, calls=%fused_computation.83 | convolution fusion | flops 910295040 | bytes 29884416 | tf_op jit(solution)/shard_map/qhd,khd->hqk/dot_general | solution.py:54
  185.9 14.6 %collective-permute-done.13 = bf16[768,256]{0,1:T(8,128)(2,1)} collective-permute-done((bf16[768,256]{0,1:T(8,128)(2,1)}, bf16[768,256]{0,1:T(8,128)(2,1)}, u32[]{:S(2)}, u32[]{:S(2)}) %collective-permute-start.13) | collective-permute-done | bytes 393248 | tf_op jit(solution)/shard_map/ppermute | solution.py:16
  200.5 19.0 %fusion.35 = f32[768,4,64]{0,2,1:T(8,128)} fusion(f32[4,2304,768]{2,1,0:T(8,128)} %fusion.55, f32[4,2304]{1,0:T(4,128)S(1)} %maximum_bitcast_fusion.1, f32[4,2304]{1,0:T(4,128)S(1)} %maximum_bitcast_fusion, pred[2304,768]{1,0:T(8,128)(4,1)} %compare_or_fusion, bf16[768,4,64]{0,2,1:T(8,128)(2,1)} %fusion.38, bf16[768,4,64]{0,2,1:T(8,128)(2,1)} %bitcast.32, ...), kind=kOutput, calls=%fused_computation.53 | convolution fusion | flops 1868759040 | bytes 33693696 | tf_op jit(solution)/shard_map/hqk,qhd->khd/dot_general | solution.py:202
  221.2 14.0 %fusion.41 = bf16[4,64,768]{2,1,0:T(8,128)(2,1)} fusion(f32[4,2304,768]{2,1,0:T(8,128)} %fusion.55, f32[4,2304]{1,0:T(4,128)} %copy-done.29, pred[2304,768]{1,0:T(8,128)(4,1)} %compare_or_fusion, bf16[768,4,64]{0,2,1:T(8,128)(2,1)} %bitcast.32, bf16[768,4,64]{0,2,1:T(8,128)(2,1)} %bitcast.31, bf16[768,4,64]{0,2,1:T(8,128)(2,1)} %bitcast.30), kind=kOutput, calls=%fused_computation.57 | convolution fusion | flops 945094656 | bytes 31690752 | tf_op jit(solution)/shard_map/hqk,qhd->khd/dot_general | solution.py:205
  236.1 2.9 multiply_subtract_fusion
  241.2 3.3 fusion.52
  250.2 4.6 add_add_fusion
  255.1 4.1 fusion.90
  261.6 5.9 fusion.97
  267.5 4.3 fusion.89
  277.3 52.5 %all-reduce.5.cloned.1.call-done = f32[768,1024]{1,0:T(8,128)} async-done(((f32[768,1024]{1,0:T(8,128)}), f32[768,1024]{1,0:T(8,128)}) %all-reduce.5.cloned.1.call-update) | async-done | bytes 3145744 | tf_op jit(solution)/shard_map/psum | solution.py:233
  329.7 3.4 fusion.91
  334.6 22.2 %all-reduce = (f32[256]{0:T(256)}, f32[256]{0:T(256)}, f32[1024]{0:T(1024)}, f32[256]{0:T(256)}) all-reduce(f32[256]{0:T(256)S(1)} %dynamic_slice.10, f32[256]{0:T(256)S(1)} %dynamic_slice.11, f32[1024]{0:T(1024)S(1)} %get-tuple-element.22, f32[256]{0:T(256)S(1)} %get-tuple-element.42), channel_id=1, replica_groups=mesh['seq'=8,'tp'=4] {'seq'}, use_global_device_ids=true, to_apply=%region_10.11 | all-reduce | flops 1792 | bytes 14336 | tf_op jit(solution)/shard_map/psum | solution.py:245
  356.8 13.4 %reduce-scatter.2.cloned.1.call-done = f32[768,256]{1,0:T(8,128)} async-done(((f32[768,1024]{1,0:T(8,128)}), f32[768,256]{1,0:T(8,128)}) %reduce-scatter.2.cloned.1.call-update) | async-done | bytes 786448 | tf_op jit(solution)/shard_map/reduce_scatter | solution.py:115
  372.2 405.1 %all-reduce.7.cloned.1.call-done = (f32[3,1024,256]{2,1,0:T(8,128)}, f32[256,1024]{1,0:T(8,128)}, f32[1024,1024]{1,0:T(8,128)}, f32[1024,1024]{1,0:T(8,128)}) async-done(((f32[3,1024,256]{2,1,0:T(8,128)}, f32[256,1024]{1,0:T(8,128)}, f32[1024,1024]{1,0:T(8,128)}, f32[1024,1024]{1,0:T(8,128)}), (f32[3,1024,256]{2,1,0:T(8,128)}, f32[256,1024]{1,0:T(8,128)}, f32[1024,1024]{1,0:T(8,128)}, ...) | async-done | bytes 12582928 | tf_op jit(solution)/shard_map/psum | solution.py:245
  777.3 3.9 copy.30
  (184 shorter events, 70.8 us)
Async XLA Ops:
  7.2 82.6 %copy-start = (bf16[1024,1024]{1,0:T(8,128)(2,1)S(1)}, bf16[1024,1024]{1,0:T(8,128)(2,1)}, u32[]{:S(2)}) copy-start(bf16[1024,1024]{1,0:T(8,128)(2,1)} %param.19) | copy-start | bytes 6291460
  7.2 28.6 %all-gather.3.cloned.1.call-start = ((), (), s32[]{:S(2)}) async-start(), calls=%async_computation.1 | async-start | bytes 1966080 | tf_op jit(solution)/shard_map/all_gather | solution.py:72
  7.9 81.9 %all-gather.5.cloned.1.call-start = ((), (), s32[]{:S(2)}) async-start(), calls=%async_computation.3 | async-start | bytes 1966080 | tf_op jit(solution)/shard_map/all_gather | solution.py:117
  8.7 18.4 %collective-permute-start.3 = (s32[768]{0:T(1024)S(1)}, s32[768]{0:T(1024)S(1)}, u32[]{:S(2)}, u32[]{:S(2)}) collective-permute-start(s32[768]{0:T(1024)S(1)} %compare_select_fusion), channel_id=1, source_target_pairs={{0,4},{4,8},{8,12},{12,16},{16,20},{20,24},{24,28},{1,5},{5,9},{9,... | collective-permute-start | bytes 9224 | tf_op jit(solution)/shard_map/ppermute | solution.py:16
  13.5 13.5 %collective-permute-start.2 = (s32[768]{0:T(1024)S(1)}, s32[768]{0:T(1024)S(1)}, u32[]{:S(2)}, u32[]{:S(2)}) collective-permute-start(s32[768]{0:T(1024)S(1)} %compare_select_fusion), channel_id=1, source_target_pairs={{0,8},{4,12},{8,16},{12,20},{16,24},{20,28},{1,9},{5,13},{9,17},{1... | collective-permute-start | bytes 9224 | tf_op jit(solution)/shard_map/ppermute | solution.py:16
  17.0 14.3 %collective-permute-start.9 = (s32[768]{0:T(1024)}, s32[768]{0:T(1024)S(1)}, u32[]{:S(2)}, u32[]{:S(2)}) collective-permute-start(s32[768]{0:T(1024)} %param.22), channel_id=1, source_target_pairs={{8,0},{12,4},{16,8},{20,12},{24,16},{28,20},{9,1},{13,5},{17,9},{2... | collective-permute-start | bytes 9224 | tf_op jit(solution)/shard_map/ppermute | solution.py:16
  18.3 13.0 %collective-permute-start.8 = (s32[768]{0:T(1024)}, s32[768]{0:T(1024)S(1)}, u32[]{:S(2)}, u32[]{:S(2)}) collective-permute-start(s32[768]{0:T(1024)} %param.22), channel_id=1, source_target_pairs={{4,0},{8,4},{12,8},{16,12},{20,16},{24,20},{28,24},{5,1},{9,5},{13... | collective-permute-start | bytes 9224 | tf_op jit(solution)/shard_map/ppermute | solution.py:16
  19.6 310.1 %all-reduce.5.cloned.1.call-start = ((), (), s32[]{:S(2)}) async-start(), calls=%async_computation.4 | async-start | bytes 6291456 | tf_op jit(solution)/shard_map/psum | solution.py:233
  49.3 50.0 %collective-permute-start.5 = (bf16[768,256]{0,1:T(8,128)(2,1)}, bf16[768,256]{0,1:T(8,128)(2,1)}, u32[]{:S(2)}, u32[]{:S(2)}) collective-permute-start(bf16[768,256]{0,1:T(8,128)(2,1)} %bitcast.13), channel_id=1, source_target_pairs={{0,4},{4,8},{8,12},{12,16},{16,20},{20,24},{24,28},{1,5},{5,9},{9,... | collective-permute-start | bytes 1179656 | tf_op jit(solution)/shard_map/ppermute | solution.py:16
  54.6 46.0 %collective-permute-start.4 = (bf16[768,256]{0,1:T(8,128)(2,1)}, bf16[768,256]{0,1:T(8,128)(2,1)}, u32[]{:S(2)}, u32[]{:S(2)}) collective-permute-start(bf16[768,256]{0,1:T(8,128)(2,1)} %bitcast.13), channel_id=1, source_target_pairs={{0,8},{4,12},{8,16},{12,20},{16,24},{20,28},{1,9},{5,13},{9,17},{1... | collective-permute-start | bytes 1179656 | tf_op jit(solution)/shard_map/ppermute | solution.py:16
  63.1 68.0 %collective-permute-start.1 = (bf16[768,256]{0,1:T(8,128)(2,1)}, bf16[768,256]{0,1:T(8,128)(2,1)}, u32[]{:S(2)}, u32[]{:S(2)}) collective-permute-start(bf16[768,256]{0,1:T(8,128)(2,1)} %bitcast.4), channel_id=1, source_target_pairs={{0,4},{4,8},{8,12},{12,16},{16,20},{20,24},{24,28},{1,5},{5,9},{9,... | collective-permute-start | bytes 1179656 | tf_op jit(solution)/shard_map/ppermute | solution.py:16
  68.3 62.7 %collective-permute-start = (bf16[768,256]{0,1:T(8,128)(2,1)}, bf16[768,256]{0,1:T(8,128)(2,1)}, u32[]{:S(2)}, u32[]{:S(2)}) collective-permute-start(bf16[768,256]{0,1:T(8,128)(2,1)} %bitcast.4), channel_id=1, source_target_pairs={{0,8},{4,12},{8,16},{12,20},{16,24},{20,28},{1,9},{5,13},{9,17},{1... | collective-permute-start | bytes 1179656 | tf_op jit(solution)/shard_map/ppermute | solution.py:16
  71.2 18.6 %copy-start.35 = (f32[1024]{0:T(1024)S(1)}, f32[1024]{0:T(1024)}, u32[]{:S(2)}) copy-start(f32[1024]{0:T(1024)} %param.18) | copy-start | bytes 12292
  71.2 96.5 %collective-permute-start.7 = (bf16[768,256]{0,1:T(8,128)(2,1)S(1)}, bf16[768,256]{0,1:T(8,128)(2,1)}, u32[]{:S(2)}, u32[]{:S(2)}) collective-permute-start(bf16[768,256]{0,1:T(8,128)(2,1)S(1)} %bitcast.130), channel_id=1, source_target_pairs={{8,0},{12,4},{16,8},{20,12},{24,16},{28,20},{9,1},{13,5},{17,9},{2... | collective-permute-start | bytes 1179656 | tf_op jit(solution)/shard_map/ppermute | solution.py:16
  99.3 70.2 %collective-permute-start.6 = (bf16[768,256]{0,1:T(8,128)(2,1)S(1)}, bf16[768,256]{0,1:T(8,128)(2,1)}, u32[]{:S(2)}, u32[]{:S(2)}) collective-permute-start(bf16[768,256]{0,1:T(8,128)(2,1)S(1)} %bitcast.131), channel_id=1, source_target_pairs={{4,0},{8,4},{12,8},{16,12},{20,16},{24,20},{28,24},{5,1},{9,5},{13... | collective-permute-start | bytes 1179656 | tf_op jit(solution)/shard_map/ppermute | solution.py:16
  114.3 15.0 %copy-start.6 = (bf16[768,1024]{1,0:T(8,128)(2,1)S(1)}, bf16[768,1024]{1,0:T(8,128)(2,1)}, u32[]{:S(2)}) copy-start(bf16[768,1024]{1,0:T(8,128)(2,1)} %all-gather.5.cloned.1.call-done) | copy-start | bytes 4718596
  114.4 15.0 %copy-start.10 = (bf16[256,1024]{1,0:T(8,128)(2,1)S(1)}, bf16[256,1024]{1,0:T(8,128)(2,1)}, u32[]{:S(2)}) copy-start(bf16[256,1024]{1,0:T(8,128)(2,1)} %param.16) | copy-start | bytes 1572868
  146.0 38.5 %collective-permute-start.15 = (f32[768,4]{0,1:T(4,128)S(1)}, f32[768,4]{0,1:T(4,128)S(1)}, u32[]{:S(2)}, u32[]{:S(2)}) collective-permute-start(f32[768,4]{0,1:T(4,128)S(1)} %bitcast_divide_fusion.2), channel_id=1, source_target_pairs={{8,0},{12,4},{16,8},{20,12},{24,16},{28,20},{9,1},{13,5},{17,9},{2... | collective-permute-start | bytes 36872 | tf_op jit(solution)/shard_map/ppermute | solution.py:16
  147.3 38.5 %collective-permute-start.14 = (f32[768,4]{0,1:T(4,128)S(1)}, f32[768,4]{0,1:T(4,128)S(1)}, u32[]{:S(2)}, u32[]{:S(2)}) collective-permute-start(f32[768,4]{0,1:T(4,128)S(1)} %bitcast_divide_fusion.2), channel_id=1, source_target_pairs={{4,0},{8,4},{12,8},{16,12},{20,16},{24,20},{28,24},{5,1},{9,5},{13... | collective-permute-start | bytes 36872 | tf_op jit(solution)/shard_map/ppermute | solution.py:16
  148.6 37.2 %collective-permute-start.11 = (f32[768,4]{0,1:T(4,128)S(1)}, f32[768,4]{0,1:T(4,128)S(1)}, u32[]{:S(2)}, u32[]{:S(2)}) collective-permute-start(f32[768,4]{0,1:T(4,128)S(1)} %get-tuple-element.48), channel_id=1, source_target_pairs={{8,0},{12,4},{16,8},{20,12},{24,16},{28,20},{9,1},{13,5},{17,9},{2... | collective-permute-start | bytes 36872 | tf_op jit(solution)/shard_map/ppermute | solution.py:16
  167.8 18.1 %collective-permute-start.10 = (f32[768,4]{0,1:T(4,128)S(1)}, f32[768,4]{0,1:T(4,128)S(1)}, u32[]{:S(2)}, u32[]{:S(2)}) collective-permute-start(f32[768,4]{0,1:T(4,128)S(1)} %get-tuple-element.48), channel_id=1, source_target_pairs={{4,0},{8,4},{12,8},{16,12},{20,16},{24,20},{28,24},{5,1},{9,5},{13... | collective-permute-start | bytes 36872 | tf_op jit(solution)/shard_map/ppermute | solution.py:16
  182.2 18.2 %collective-permute-start.13 = (bf16[768,256]{0,1:T(8,128)(2,1)}, bf16[768,256]{0,1:T(8,128)(2,1)}, u32[]{:S(2)}, u32[]{:S(2)}) collective-permute-start(bf16[768,256]{0,1:T(8,128)(2,1)} %get-tuple-element.56), channel_id=1, source_target_pairs={{8,0},{12,4},{16,8},{20,12},{24,16},{28,20},{9,1},{13,5},{17,9},{2... | collective-permute-start | bytes 1179656 | tf_op jit(solution)/shard_map/ppermute | solution.py:16
  184.5 15.9 %collective-permute-start.12 = (bf16[768,256]{0,1:T(8,128)(2,1)}, bf16[768,256]{0,1:T(8,128)(2,1)}, u32[]{:S(2)}, u32[]{:S(2)}) collective-permute-start(bf16[768,256]{0,1:T(8,128)(2,1)} %get-tuple-element.56), channel_id=1, source_target_pairs={{4,0},{8,4},{12,8},{16,12},{20,16},{24,20},{28,24},{5,1},{9,5},{13... | collective-permute-start | bytes 1179656 | tf_op jit(solution)/shard_map/ppermute | solution.py:16
  185.9 33.6 %copy-start.29 = (f32[4,2304]{1,0:T(4,128)}, f32[4,2304]{1,0:T(4,128)S(1)}, u32[]{:S(2)}) copy-start(f32[4,2304]{1,0:T(4,128)S(1)} %maximum_bitcast_fusion) | copy-start | bytes 110596
  254.9 115.3 %reduce-scatter.2.cloned.1.call-start = ((), (), s32[]{:S(2)}) async-start(), calls=%async_computation.2 | async-start | bytes 3932160 | tf_op jit(solution)/shard_map/reduce_scatter | solution.py:115
  261.5 515.8 %all-reduce.7.cloned.1.call-start = ((), (), s32[]{:S(2)}) async-start(), calls=%async_computation.5 | async-start | bytes 25165824 | tf_op jit(solution)/shard_map/psum | solution.py:245
  277.2 52.5 %copy-start.25 = (f32[768]{0:T(1024)S(1)}, f32[768]{0:T(1024)}, u32[]{:S(2)}) copy-start(f32[768]{0:T(1024)} %copy-done.24) | copy-start | bytes 9220
  277.2 52.5 %copy-start.27 = (f32[768]{0:T(1024)S(1)}, f32[768]{0:T(1024)}, u32[]{:S(2)}) copy-start(f32[768]{0:T(1024)} %copy-done.26) | copy-start | bytes 9220
  277.2 52.5 %copy-start.31 = (f32[1024]{0:T(1024)S(1)}, f32[1024]{0:T(1024)}, u32[]{:S(2)}) copy-start(f32[1024]{0:T(1024)} %param.13) | copy-start | bytes 12292
  277.2 56.1 %copy-start.16 = (bf16[768,256]{1,0:T(8,128)(2,1)S(1)}, bf16[768,256]{1,0:T(8,128)(2,1)}, u32[]{:S(2)}) copy-start(bf16[768,256]{1,0:T(8,128)(2,1)} %param.21) | copy-start | bytes 1179652
  277.2 93.0 %copy-start.14 = (bf16[768,256]{1,0:T(8,128)(2,1)S(1)}, bf16[768,256]{1,0:T(8,128)(2,1)}, u32[]{:S(2)}) copy-start(bf16[768,256]{1,0:T(8,128)(2,1)} %param.12) | copy-start | bytes 1179652
  277.2 93.0 %copy-start.33 = (f32[256]{0:T(256)S(1)}, f32[256]{0:T(256)}, u32[]{:S(2)}) copy-start(f32[256]{0:T(256)} %param.20) | copy-start | bytes 3076
  (28 other events, 170.9 us)
Sparse Core Ops, SparseCore 0:
  9.6 22.5 all-gather.2
  33.7 19.8 all-gather.4
  255.0 74.6 all-reduce.4
  332.1 38.0 reduce-scatter.1
  376.7 400.5 all-reduce.6
where the time goes:
time: 797 us; the launch traced here: 795 us
  waiting for transfers between devices  486 us (61%)
  matrix products  143 us (18%)
  starting transfers between devices  51.7 us (6%)
  other arithmetic  49.1 us (6%)
  local copies, waits for them, and re-layouts  27.8 us (3%)
  blocking collectives  22.2 us (3%)
  between operations  14.7 us (2%)
    psum x1, waiting for transfers between devices, shards(): lax.psum((grad_qkv, grad_wo, grad_win, grad_bin, grad_wout, grad_bout, gr...  405 us
    psum x1, waiting for transfers between devices, shards(): grad_norm = lax.psum(grad_norm_part, 'tp')  52.5 us
    ppermute x16, starting transfers between devices, passed_along(): lax.ppermute(value, axis, [(source, source + steps) for source in range(l...  51.3 us
    dot_general x2, matrix products, base_two(): jnp.einsum('qhd,khd->hqk', query_rot, key_part, preferred_element_type=jn...  25.7 us
    psum x1, blocking collectives, shards(): lax.psum((grad_qkv, grad_wo, grad_win, grad_bin, grad_wout, grad_bout, gr...  22.2 us
    dot_general x1, matrix products, shards(): jnp.einsum('hqk,qhd->khd', logit_back, query_heads, preferred_element_typ...  19 us
    dot_general x1, matrix products, shards(): jnp.einsum('hqk,khd->qhd', grad_logit, key_heads, preferred_element_type=...  17.9 us
  transfers between devices with their start and end apart: 21, of which 4 were waited for; matrix products, arithmetic and copies ran while one was open for 19% of the time, Pallas kernels for 0%

commit v1 on v0

--- a/solution.py
+++ b/solution.py
@@ -1,6 +1,10 @@
+import functools
+
 import jax
 import jax.numpy as jnp
 from jax import lax
+from jax.experimental import pallas as pl
+from jax.experimental.pallas import tpu as pltpu
 from jax.sharding import PartitionSpec as P
 
 PACK = 1024
@@ -8,6 +12,448 @@
 
 LOG2E = 1.4426950408889634
 EPSILON = 1e-05
+
+
+MESH = pl.DeviceIdType.MESH
+
+
+class Ring:
+    def __init__(self, seq_count):
+        self.count = seq_count
+        self.m = seq_count // 2
+        self.s = lax.axis_index("seq")
+        self.t = lax.axis_index("tp")
+        self.z = self.s // 2
+        self.x = self.s % 2
+        low = (self.z < self.m // 2).astype(jnp.int32)
+        self.near = low
+        self.far = 1 - low
+
+    def at(self, z, x):
+        return (z * 2 + x, self.t)
+
+    def peer(self):
+        return self.at(self.z, 1 - self.x)
+
+    def step(self, piece, sign):
+        return self.at(self.z + sign * (2 * piece - 1), self.x)
+
+    def first(self, piece):
+        return self.z == (1 - piece) * (self.m - 1)
+
+    def last(self, piece):
+        return self.z == piece * (self.m - 1)
+
+
+def aligned(value):
+    return pl.multiple_of(value, 16)
+
+
+def add_rows(acc, acc_first, got, rows):
+    step = 16 if rows % 32 else 32
+
+    def body(i, carry):
+        at = pl.ds(aligned(acc_first + i * step), step)
+        here = pl.ds(aligned(i * step), step)
+        acc[at, :] = (acc[at, :].astype(jnp.float32) + got[here, :].astype(jnp.float32)).astype(
+            acc.dtype
+        )
+        return carry
+
+    lax.fori_loop(0, rows // step, body, 0)
+
+
+class Unit:
+    def __init__(self, ring, index, part, out, out_first, rows, pair_buf, line_buf, send, recv, own):
+        self.r, self.u = ring, index
+        self.part, self.out, self.out_first, self.rows = part, out, out_first, rows
+        self.pair_buf, self.line_buf = pair_buf, line_buf
+        self.send, self.recv, self.own = send, recv, own
+
+    def copy(self, src, dst, kind, to):
+        return pltpu.make_async_remote_copy(
+            src_ref=src,
+            dst_ref=dst,
+            send_sem=self.send.at[self.u, kind],
+            recv_sem=self.recv.at[self.u, kind],
+            device_id=to,
+            device_id_type=MESH,
+        )
+
+    def p(self, first, rows):
+        return self.part.at[pl.ds(aligned(first), rows)]
+
+    def o(self, first, rows):
+        return self.out.at[pl.ds(aligned(self.out_first + first), rows)]
+
+    def keep(self, first, rows):
+        return pltpu.make_async_copy(self.p(first, rows), self.o(first, rows), self.own.at[self.u])
+
+
+class PairFirst(Unit):
+    def pair(self):
+        half = self.rows // 2
+        return self.copy(self.p((1 - self.r.x) * half, half), self.pair_buf, 0, self.r.peer())
+
+    def first_row(self, piece, member):
+        return member * (self.rows // 2) + piece * (self.rows // 4)
+
+    def line(self, piece):
+        quarter = self.rows // 4
+        return self.copy(
+            self.p(self.first_row(piece, self.r.x), quarter),
+            self.line_buf.at[piece],
+            1 + piece,
+            self.r.step(piece, 1),
+        )
+
+    def back(self, piece, origin):
+        quarter = self.rows // 4
+        row = self.first_row(piece, self.r.x)
+        src = self.p(row, quarter) if origin else self.o(row, quarter)
+        return self.copy(src, self.o(row, quarter), 3 + piece, self.r.step(piece, -1))
+
+    def over(self, piece, origin):
+        quarter = self.rows // 4
+        row = self.first_row(piece, self.r.x)
+        src = self.p(row, quarter) if origin else self.o(row, quarter)
+        return self.copy(src, self.o(row, quarter), 5 + piece, self.r.peer())
+
+    def start(self):
+        self.pair().start()
+
+    def paired(self):
+        half = self.rows // 2
+        self.pair().wait_recv()
+        add_rows(self.part, self.r.x * half, self.pair_buf, half)
+        piece = self.r.near
+
+        @pl.when(self.r.first(piece))
+        def _():
+            self.line(piece).start()
+
+    def chain_near(self):
+        piece = self.r.near
+
+        @pl.when(jnp.logical_not(self.r.first(piece)))
+        def _():
+            self.line(piece).wait_recv()
+            add_rows(
+                self.part, self.first_row(piece, self.r.x), self.line_buf.at[piece], self.rows // 4
+            )
+            self.line(piece).start()
+
+    def chain_far(self):
+        piece = self.r.far
+        self.line(piece).wait_recv()
+        add_rows(self.part, self.first_row(piece, self.r.x), self.line_buf.at[piece], self.rows // 4)
+
+        @pl.when(jnp.logical_not(self.r.last(piece)))
+        def _():
+            self.line(piece).start()
+
+        @pl.when(self.r.last(piece))
+        def _():
+            self.back(piece, True).start()
+            self.over(piece, True).start()
+            self.keep(self.first_row(piece, self.r.x), self.rows // 4).start()
+
+    def exchanged(self):
+        pass
+
+    def back_near(self):
+        piece = self.r.far
+
+        @pl.when(jnp.logical_not(self.r.last(piece)))
+        def _():
+            self.back(piece, False).wait_recv()
+            self.back(piece, False).start()
+            self.over(piece, False).start()
+
+    def back_far(self):
+        piece = self.r.near
+        self.back(piece, False).wait_recv()
+
+        @pl.when(jnp.logical_not(self.r.first(piece)))
+        def _():
+            self.back(piece, False).start()
+
+        self.over(piece, False).start()
+
+    def finish(self):
+        quarter = self.rows // 4
+        for piece in (0, 1):
+            row = self.first_row(piece, 1 - self.r.x)
+            self.copy(self.o(row, quarter), self.o(row, quarter), 5 + piece, self.r.peer()).wait_recv()
+        self.pair().wait_send()
+        for piece in (0, 1):
+
+            @pl.when(jnp.logical_not(self.r.last(piece)))
+            def _():
+                self.line(piece).wait_send()
+
+            @pl.when(jnp.logical_not(self.r.first(piece)))
+            def _():
+                self.back(piece, False).wait_send()
+
+            self.over(piece, False).wait_send()
+
+        @pl.when(self.r.last(self.r.far))
+        def _():
+            self.keep(self.first_row(self.r.far, self.r.x), quarter).wait()
+
+
+class LineFirst(Unit):
+    def line(self, piece):
+        half = self.rows // 2
+        return self.copy(
+            self.p(piece * half, half), self.line_buf.at[piece], 1 + piece, self.r.step(piece, 1)
+        )
+
+    def row_of(self, piece, member):
+        return piece * (self.rows // 2) + member * (self.rows // 4)
+
+    def pair(self, piece):
+        quarter = self.rows // 4
+        return self.copy(
+            self.p(self.row_of(piece, 1 - self.r.x), quarter), self.pair_buf, 0, self.r.peer()
+        )
+
+    def over(self, piece, member, origin):
+        quarter = self.rows // 4
+        row = self.row_of(piece, member)
+        src = self.p(row, quarter) if origin else self.o(row, quarter)
+        return self.copy(src, self.o(row, quarter), 3, self.r.peer())
+
+    def back(self, piece, member, origin):
+        quarter = self.rows // 4
+        row = self.row_of(piece, member)
+        src = self.p(row, quarter) if origin else self.o(row, quarter)
+        return self.copy(src, self.o(row, quarter), 4 + 2 * piece + member, self.r.step(piece, -1))
+
+    def start(self):
+        piece = self.r.near
+
+        @pl.when(self.r.first(piece))
+        def _():
+            self.line(piece).start()
+
+    def paired(self):
+        pass
+
+    def chain_near(self):
+        piece = self.r.near
+
+        @pl.when(jnp.logical_not(self.r.first(piece)))
+        def _():
+            self.line(piece).wait_recv()
+            add_rows(self.part, piece * (self.rows // 2), self.line_buf.at[piece], self.rows // 2)
+            self.line(piece).start()
+
+    def chain_far(self):
+        piece = self.r.far
+        self.line(piece).wait_recv()
+        add_rows(self.part, piece * (self.rows // 2), self.line_buf.at[piece], self.rows // 2)
+
+        @pl.when(jnp.logical_not(self.r.last(piece)))
+        def _():
+            self.line(piece).start()
+
+        @pl.when(self.r.last(piece))
+        def _():
+            self.pair(piece).start()
+
+    def exchanged(self):
+        piece = self.r.far
+        quarter = self.rows // 4
+
+        @pl.when(self.r.last(piece))
+        def _():
+            self.pair(piece).wait_recv()
+            row = self.row_of(piece, self.r.x)
+            add_rows(self.part, row, self.pair_buf, quarter)
+            self.over(piece, self.r.x, True).start()
+            self.back(piece, self.r.x, True).start()
+            self.keep(row, quarter).start()
+
+    def back_near(self):
+        piece = self.r.far
+        other = 1 - self.r.x
+
+        @pl.when(self.r.last(piece))
+        def _():
+            self.over(piece, other, False).wait_recv()
+            self.back(piece, other, False).start()
+
+        @pl.when(jnp.logical_not(self.r.last(piece)))
+        def _():
+            for member in (self.r.x, other):
+                self.back(piece, member, False).wait_recv()
+                self.back(piece, member, False).start()
+
+    def back_far(self):
+        piece = self.r.near
+        for member in (self.r.x, 1 - self.r.x):
+            self.back(piece, member, False).wait_recv()
+
+            @pl.when(jnp.logical_not(self.r.first(piece)))
+            def _():
+                self.back(piece, member, False).start()
+
+    def finish(self):
+        quarter = self.rows // 4
+        for piece in (0, 1):
+
+            @pl.when(jnp.logical_not(self.r.last(piece)))
+            def _():
+                self.line(piece).wait_send()
+
+            @pl.when(jnp.logical_not(self.r.first(piece)))
+            def _():
+                for member in (0, 1):
+                    self.back(piece, member, False).wait_send()
+
+        piece = self.r.far
+
+        @pl.when(self.r.last(piece))
+        def _():
+            self.pair(piece).wait_send()
+            self.over(piece, self.r.x, False).wait_send()
+            self.keep(self.row_of(piece, self.r.x), quarter).wait()
+
+
+ROLES = ("start", "paired", "chain_near", "chain_far", "exchanged", "back_near", "back_far")
+
+
+def greet(ring, with_tp):
+    barrier = pltpu.get_barrier_semaphore()
+    s, t, count = ring.s, ring.t, ring.count
+
+    def signal(to):
+        pl.semaphore_signal(barrier, inc=1, device_id=to, device_id_type=MESH)
+
+    total = jnp.int32(0)
+    bit = 1
+    while bit < count:
+        signal((s + bit - 2 * bit * ((s // bit) % 2), t))
+        total = total + 1
+        bit *= 2
+    for sign in (-1, 1):
+        ok = (ring.z + sign >= 0) & (ring.z + sign < ring.m)
+
+        @pl.when(ok)
+        def _():
+            signal(ring.at(ring.z + sign, ring.x))
+
+        total = total + ok.astype(jnp.int32)
+    pl.semaphore_wait(barrier, total)
+
+
+def vector_sum(ring, vec, got, send, recv):
+    bit, level = 1, 0
+    copies = []
+    while bit < ring.count:
+        other = ring.s + bit - 2 * bit * ((ring.s // bit) % 2)
+        copy = pltpu.make_async_remote_copy(
+            src_ref=vec.at[level],
+            dst_ref=got.at[level],
+            send_sem=send.at[level],
+            recv_sem=recv.at[level],
+            device_id=(other, ring.t),
+            device_id_type=MESH,
+        )
+        copy.start()
+        copy.wait_recv()
+        vec[level + 1] = vec[level] + got[level]
+        copies.append(copy)
+        bit *= 2
+        level += 1
+    return copies
+
+
+def sum_kernel(count, wout_in, win_in, wo_in, qkv_in, vec_in, wout, win, wo, qkv, vec_out,
+               wide, tall, pair_wide, line_wide, pair_tall, line_tall, pair_wide2, line_wide2,
+               pair_tall2, line_tall2, vec, got, send, recv, own, vsend, vrecv, lsem):
+    ring = Ring(count)
+    loads = []
+    for i, (ref, first, rows) in enumerate(((wout_in, 0, 1024), (win_in, 1024, 1024), (wo_in, 2048, 256))):
+        loads.append(pltpu.make_async_copy(ref, wide.at[pl.ds(first, rows)], lsem.at[i]))
+    loads.append(pltpu.make_async_copy(qkv_in, tall, lsem.at[3]))
+    for load in loads:
+        load.start()
+    greet(ring, False)
+    for load in loads:
+        load.wait()
+    units = []
+    for u in range(12):
+        if u < 9:
+            out, first = ((wout, u * 256) if u < 4 else (win, (u - 4) * 256) if u < 8 else (wo, 0))
+            args = (wide.at[pl.ds(u * 256, 256)], out, first, 256)
+            bufs = (pair_wide, line_wide) if u % 2 == 0 else (pair_wide2, line_wide2)
+            slot = u // 2
+        else:
+            args = (tall.at[u - 9], qkv.at[u - 9], 0, 1024)
+            bufs = (pair_tall, line_tall) if u % 2 == 0 else (pair_tall2, line_tall2)
+            slot = (u - 9) // 2
+        kind = PairFirst if u % 2 == 0 else LineFirst
+        units.append(kind(ring, u, *args, bufs[0].at[slot], bufs[1].at[slot], send, recv, own))
+    for unit in units:
+        unit.start()
+    vec[0] = vec_in[...]
+    copies = vector_sum(ring, vec, got, vsend, vrecv)
+    vec_out[...] = vec[len(copies)]
+    for tick in range(6 + len(ROLES) - 1):
+        for late, role in enumerate(ROLES[1:]):
+            k = tick - late
+            if 0 <= k < 6:
+                getattr(units[2 * k + 1], role)()
+                getattr(units[2 * k], role)()
+    for unit in units:
+        unit.finish()
+    for copy in copies:
+        copy.wait_send()
+
+
+def sum_over_seq(count, wout, win, wo, qkv, vec):
+    levels = count.bit_length() - 1
+    any_spec = pl.BlockSpec(memory_space=pl.ANY)
+    vm = pl.BlockSpec(memory_space=pltpu.VMEM)
+    bf = jnp.bfloat16
+    return pl.pallas_call(
+        functools.partial(sum_kernel, count),
+        out_shape=[
+            jax.ShapeDtypeStruct(wout.shape, bf),
+            jax.ShapeDtypeStruct(win.shape, bf),
+            jax.ShapeDtypeStruct(wo.shape, bf),
+            jax.ShapeDtypeStruct(qkv.shape, bf),
+            jax.ShapeDtypeStruct(vec.shape, jnp.float32),
+        ],
+        in_specs=[any_spec] * 4 + [vm],
+        out_specs=[any_spec] * 4 + [vm],
+        scratch_shapes=[
+            pltpu.VMEM((2304, 1024), bf),
+            pltpu.VMEM((3, 1024, 256), bf),
+            pltpu.VMEM((5, 128, 1024), bf),
+            pltpu.VMEM((5, 2, 64, 1024), bf),
+            pltpu.VMEM((2, 512, 256), bf),
+            pltpu.VMEM((2, 2, 256, 256), bf),
+            pltpu.VMEM((4, 64, 1024), bf),
+            pltpu.VMEM((4, 2, 128, 1024), bf),
+            pltpu.VMEM((2, 256, 256), bf),
+            pltpu.VMEM((2, 2, 512, 256), bf),
+            pltpu.VMEM((levels + 1,) + vec.shape, jnp.float32),
+            pltpu.VMEM((levels,) + vec.shape, jnp.float32),
+            pltpu.SemaphoreType.DMA((12, 8)),
+            pltpu.SemaphoreType.DMA((12, 8)),
+            pltpu.SemaphoreType.DMA((12,)),
+            pltpu.SemaphoreType.DMA((levels,)),
+            pltpu.SemaphoreType.DMA((levels,)),
+            pltpu.SemaphoreType.DMA((4,)),
+        ],
+        compiler_params=pltpu.CompilerParams(
+            collective_id=0, has_side_effects=True, vmem_limit_bytes=48 * 2**20
+        ),
+    )(wout, win, wo, qkv, vec)
 
 
 def passed_along(value, axis, steps):
@@ -242,20 +688,26 @@
     grad_input = lax.dynamic_slice_in_dim(
         grad_full, feature_first, width_local, 1
     ) + grad_out.astype(jnp.float32)
-    totals_out = lax.psum(
-        (grad_qkv, grad_wo, grad_win, grad_bin, grad_wout, grad_bout, grad_gain, grad_bias), "seq"
-    )
+    bf = jnp.bfloat16
+    vec = jnp.zeros((8, 1024), jnp.float32)
+    vec = vec.at[0].set(grad_bin).at[1, :256].set(grad_gain).at[1, 256:512].set(grad_bias)
+    vec = vec.at[1, 512:768].set(grad_bout)
+    wout, win, wo, qkv, vec = sum_over_seq(
+        lax.axis_size("seq"), grad_wout.astype(bf), grad_win.astype(bf), grad_wo.astype(bf),
+        grad_qkv.astype(bf), vec
+    )
+    f32 = jnp.float32
     return (
         mixed,
         grad_input,
-        totals_out[6],
-        totals_out[7],
-        totals_out[0],
-        totals_out[1],
-        totals_out[2],
-        totals_out[3],
-        totals_out[4],
-        totals_out[5],
+        vec[1, :256],
+        vec[1, 256:512],
+        qkv.astype(f32),
+        wo.astype(f32),
+        win.astype(f32),
+        vec[0],
+        wout.astype(f32),
+        vec[1, 512:768],
     )
 
 

time: 797 us -> 556 us (0.70)
  waiting for transfers between devices: 486 us -> 68.5 us
  Pallas kernels: 0 us -> 189 us
  blocking collectives: 22.2 us -> 0 us
  other arithmetic: 49.1 us -> 61.7 us
    psum x1 -> x0, waiting for transfers between devices: 405 us -> none  [shards(): lax.psum((grad_qkv, grad_wo, grad_win, grad_bin, grad_wout, grad_bout, gr...]
    pallas_call x0 -> x1, Pallas kernels: none -> 189 us  [sum_over_seq(): pl.pallas_call(functools.partial(sum_kernel, count), out_shape=[jax.Shape...]
    psum x1 -> x0, blocking collectives: 22.2 us -> none  [shards(): lax.psum((grad_qkv, grad_wo, grad_win, grad_bin, grad_wout, grad_bout, gr...]
    reduce_scatter x1, waiting for transfers between devices: 13.4 us -> 0.01 us  [shards(): summed = lax.psum_scatter(branch, 'tp', scatter_dimension=1, tiled=True)]
    convert_element_type x0 -> x4, other arithmetic: none -> 7.97 us  [the longest x1 2.48 us: shards(): win.astype(f32)]
  transfers between devices with their start and end apart: 21 -> 20, of which waited for: 4 -> 2; matrix products, arithmetic and copies ran while one was open for 19% -> 30% of each run, Pallas kernels for 0% -> 34%
where the time goes in v1:
time: 556 us; the launch traced here: 548 us
  Pallas kernels  189 us (34%)
  matrix products  141 us (25%)
  waiting for transfers between devices  68.5 us (12%)
  other arithmetic  61.7 us (11%)
  starting transfers between devices  49.4 us (9%)
  local copies, waits for them, and re-layouts  23.3 us (4%)
  between operations  14.9 us (3%)
    pallas_call x1, Pallas kernels, sum_over_seq(): pl.pallas_call(functools.partial(sum_kernel, count), out_shape=[jax.Shape...  189 us
    psum x1, waiting for transfers between devices, shards(): grad_norm = lax.psum(grad_norm_part, 'tp')  54.5 us
    ppermute x16, starting transfers between devices, passed_along(): lax.ppermute(value, axis, [(source, source + steps) for source in range(l...  49 us
    dot_general x2, matrix products, base_two(): jnp.einsum('qhd,khd->hqk', query_rot, key_part, preferred_element_type=jn...  25.7 us
    dot_general x1, matrix products, shards(): jnp.einsum('hqk,qhd->khd', logit_back, query_heads, preferred_element_typ...  19 us
    dot_general x1, matrix products, shards(): jnp.einsum('hqk,khd->qhd', grad_logit, key_heads, preferred_element_type=...  17.9 us
    reduce_sum x1, other arithmetic, shards(): totals = jnp.sum(weight, 2)  15 us
    dot_general x1, matrix products, shards(): jnp.einsum('hqk,khd->qhd', weight.astype(jnp.bfloat16), value_heads, pref...  14.3 us
  transfers between devices with their start and end apart: 20, of which 2 were waited for; matrix products, arithmetic and copies ran while one was open for 30% of the time, Pallas kernels for 34%

profile of v1, /device:TPU:0, one launch (start us, length us, event | category | flops | bytes accessed | tf_op | source)
XLA Modules:
  0.0 547.5 jit_solution(16320777260115547403)
XLA Ops:
  8.7 4.8 collective-permute-start.3
  13.5 3.5 collective-permute-start.2
  26.5 4.2 compare_or_fusion.1
  30.7 4.4 compare_or_fusion
  49.8 5.3 collective-permute-start.5
  55.1 4.6 collective-permute-start.4
  60.7 2.9 fusion.38
  63.6 5.1 collective-permute-start.1
  68.7 2.8 collective-permute-start
  74.8 5.5 %fusion.97 = f32[768,1024]{1,0:T(8,128)} fusion(bf16[768,1024]{1,0:T(8,128)(2,1)} %copy-done.11, bf16[1024,1024]{1,0:T(8,128)(2,1)} %param.25), kind=kOutput, calls=%fused_computation.164 | convolution fusion | flops 1610612736 | bytes 6815744 | tf_op jit(solution)/shard_map/dot_general | solution.py:556
  80.3 6.5 %convert_reduce_fusion.1 = (f32[1024]{0:T(1024)}, bf16[768,1024]{1,0:T(8,128)(2,1)S(1)}) fusion(f32[768,1024]{1,0:T(8,128)} %fusion.97, f32[1024]{0:T(1024)S(1)} %copy-done.36, bf16[768,1024]{1,0:T(8,128)(2,1)} %all-gather.5.cloned.1.call-done, bf16[1024,1024]{1,0:T(8,128)(2,1)S(1)} %copy-done), kind=kOutput, calls=%fused_computation.34 | convolution fusion | flops 1628699648 | bytes 8396800 | tf_op jit(solution)/shard_map/dot_general | solution.py:570
  86.8 3.5 fusion.98
  91.7 13.7 %select_reduce_fusion = (f32[4,768]{1,0:T(4,128)S(1)}, f32[4,768,2304]{2,1,0:T(8,128)}) fusion(pred[768,2304]{1,0:T(8,128)(4,1)S(1)} %copy-done.4, bf16[768,4,64]{0,2,1:T(8,128)(2,1)} %maximum_convert_fusion.1, bf16[768,4,64]{0,2,1:T(8,128)(2,1)} %bitcast.15, bf16[768,4,64]{0,2,1:T(8,128)(2,1)} %bitcast.14, bf16[768,4,32]{0,2,1:T(8,128)(2,1)S(1)} %slice.169, ...), kind=kOutput, calls=%fused_computation.4 | convolution fusion | flops 931525632 | bytes 31666176 | tf_op jit(solution)/shard_map/qhd,khd->hqk/dot_general | solution.py:500
  105.4 15.0 %fusion.12 = f32[4,768]{1,0:T(4,128)S(1)} fusion(f32[4,768]{1,0:T(4,128)S(1)} %get-tuple-element.102, f32[4,768,2304]{2,1,0:T(8,128)} %get-tuple-element.107, pred[768,2304]{1,0:T(8,128)(4,1)S(1)} %copy-done.4), kind=kLoop, calls=%fused_computation.15 | loop fusion | flops 35386368 | bytes 30105600 | tf_op jit(solution)/shard_map/reduce_sum | solution.py:550
  122.1 14.3 %multiply_reduce_fusion.2 = (f32[768,4]{0,1:T(4,128)S(1)}, bf16[768,4,64]{0,2,1:T(8,128)(2,1)}) fusion(f32[768,256]{0,1:T(8,128)} %get-tuple-element.110, f32[768,4]{0,1:T(4,128)S(1)} %bitcast.149, f32[4,768]{1,0:T(4,128)S(1)} %get-tuple-element.102, f32[4,768,2304]{2,1,0:T(8,128)} %get-tuple-element.107, pred[768,2304]{1,0:T(8,128)(4,1)} %compare_or_fusion.1, ...), kind=kOutput, calls=%fused_computation.81 | convolution fusion | flops 945681408 | bytes 32477184 | tf_op jit(solution)/shard_map/hqk,khd->qhd/dot_general | solution.py:551
  142.2 17.9 %fusion.37 = f32[768,4,64]{0,2,1:T(8,128)} fusion(f32[4,768]{1,0:T(4,128)} %bitcast_divide_fusion.1, f32[4,768]{1,0:T(4,128)S(1)} %get-tuple-element.102, f32[4,768,2304]{2,1,0:T(8,128)} %get-tuple-element.107, pred[768,2304]{1,0:T(8,128)(4,1)} %compare_or_fusion.1, bf16[768,4,64]{0,2,1:T(8,128)(2,1)} %maximum_convert_fusion.1, ...), kind=kOutput, calls=%fused_computation.58 | convolution fusion | flops 1869152256 | bytes 34050048 | tf_op jit(solution)/shard_map/hqk,khd->qhd/dot_general | solution.py:613
  160.1 11.1 %collective-permute-start.10 = (f32[768,4]{0,1:T(4,128)S(1)}, f32[768,4]{0,1:T(4,128)S(1)}, u32[]{:S(2)}, u32[]{:S(2)}) collective-permute-start(f32[768,4]{0,1:T(4,128)S(1)} %get-tuple-element.101), channel_id=1, source_target_pairs={{4,0},{8,4},{12,8},{16,12},{20,16},{24,20},{28,24},{5,1},{9,5},{13... | collective-permute-start | bytes 36872 | tf_op jit(solution)/shard_map/ppermute | solution.py:462
  171.2 11.9 %fusion.58 = f32[4,2304,768]{2,1,0:T(8,128)} fusion(bf16[768,4,64]{0,2,1:T(8,128)(2,1)} %bitcast.26, bf16[768,4,64]{0,2,1:T(8,128)(2,1)} %bitcast.24, bf16[768,4,64]{0,2,1:T(8,128)(2,1)S(1)} %maximum_convert_fusion, bf16[768,4,32]{0,2,1:T(8,128)(2,1)S(1)} %slice.173, bf16[768,4,32]{0,2,1:T(8,128)(2,1)S(1)} %reshape.605), kind=kOutput, calls=%fused_computation.89 | convolution fusion | flops 910295040 | bytes 29884416 | tf_op jit(solution)/shard_map/qhd,khd->hqk/dot_general | solution.py:500
  189.0 13.2 %collective-permute-done.13 = bf16[768,256]{0,1:T(8,128)(2,1)} collective-permute-done((bf16[768,256]{0,1:T(8,128)(2,1)}, bf16[768,256]{0,1:T(8,128)(2,1)}, u32[]{:S(2)}, u32[]{:S(2)}) %collective-permute-start.13) | collective-permute-done | bytes 393248 | tf_op jit(solution)/shard_map/ppermute | solution.py:462
  202.1 19.0 %fusion.35 = f32[768,4,64]{0,2,1:T(8,128)} fusion(f32[4,2304,768]{2,1,0:T(8,128)} %fusion.58, f32[4,2304]{1,0:T(4,128)S(1)} %maximum_bitcast_fusion.1, f32[4,2304]{1,0:T(4,128)S(1)} %maximum_bitcast_fusion, pred[2304,768]{1,0:T(8,128)(4,1)} %compare_or_fusion, bf16[768,4,64]{0,2,1:T(8,128)(2,1)} %fusion.38, bf16[768,4,64]{0,2,1:T(8,128)(2,1)} %bitcast.32, ...), kind=kOutput, calls=%fused_computation.56 | convolution fusion | flops 1868759040 | bytes 33693696 | tf_op jit(solution)/shard_map/hqk,qhd->khd/dot_general | solution.py:648
  222.8 14.0 %fusion.41 = bf16[4,64,768]{2,1,0:T(8,128)(2,1)} fusion(f32[4,2304,768]{2,1,0:T(8,128)} %fusion.58, f32[4,2304]{1,0:T(4,128)} %copy-done.29, pred[2304,768]{1,0:T(8,128)(4,1)} %compare_or_fusion, bf16[768,4,64]{0,2,1:T(8,128)(2,1)} %bitcast.32, bf16[768,4,64]{0,2,1:T(8,128)(2,1)} %bitcast.31, bf16[768,4,64]{0,2,1:T(8,128)(2,1)} %bitcast.30), kind=kOutput, calls=%fused_computation.60 | convolution fusion | flops 945094656 | bytes 31690752 | tf_op jit(solution)/shard_map/hqk,qhd->khd/dot_general | solution.py:651
  242.2 3.3 fusion.55
  251.3 4.6 add_add_fusion
  256.7 4.0 fusion.92
  263.7 5.3 convolution_convert_fusion.win_in
  269.0 3.6 convolution_convert_fusion.1.wout_in
  276.5 54.5 %all-reduce.3.cloned.1.call-done = f32[768,1024]{1,0:T(8,128)} async-done(((f32[768,1024]{1,0:T(8,128)}), f32[768,1024]{1,0:T(8,128)}) %all-reduce.3.cloned.1.call-update) | async-done | bytes 3145744 | tf_op jit(solution)/shard_map/psum | solution.py:679
  331.0 5.0 fusion.93
  336.7 2.6 convert_reduce_fusion.2
  340.9 188.6 %shard_map.195 = (bf16[1024,1024]{1,0:T(8,128)(2,1)}, bf16[1024,1024]{1,0:T(8,128)(2,1)}, bf16[256,1024]{1,0:T(8,128)(2,1)S(1)}, bf16[3,1024,256]{2,1,0:T(8,128)(2,1)S(1)}, f32[8,1024]{1,0:T(8,128)S(1)}) custom-call(bf16[1024,1024]{1,0:T(8,128)(2,1)} %convolution_convert_fusion.1.wout_in, bf16[1024,1024]{1,0:T(8,128)(2,1)} %convolution_convert_fusion.win_in, ...), custom_call_target="tpu_custom_call" | custom-call | tf_op jit(solution)/shard_map/pallas_call | solution.py:422
  532.5 2.5 convert_element_type.187
  535.6 2.5 convert_element_type.188
  (191 shorter events, 72.7 us)
Async XLA Ops:
  7.2 73.1 %copy-start = (bf16[1024,1024]{1,0:T(8,128)(2,1)S(1)}, bf16[1024,1024]{1,0:T(8,128)(2,1)}, u32[]{:S(2)}) copy-start(bf16[1024,1024]{1,0:T(8,128)(2,1)} %param.27) | copy-start | bytes 6291460
  7.2 28.0 %all-gather.3.cloned.1.call-start = ((), (), s32[]{:S(2)}) async-start(), calls=%async_computation.1 | async-start | bytes 1966080 | tf_op jit(solution)/shard_map/all_gather | solution.py:518
  7.9 72.4 %all-gather.5.cloned.1.call-start = ((), (), s32[]{:S(2)}) async-start(), calls=%async_computation.3 | async-start | bytes 1966080 | tf_op jit(solution)/shard_map/all_gather | solution.py:563
  8.7 17.7 %collective-permute-start.3 = (s32[768]{0:T(1024)S(1)}, s32[768]{0:T(1024)S(1)}, u32[]{:S(2)}, u32[]{:S(2)}) collective-permute-start(s32[768]{0:T(1024)S(1)} %compare_select_fusion), channel_id=1, source_target_pairs={{0,4},{4,8},{8,12},{12,16},{16,20},{20,24},{24,28},{1,5},{5,9},{9,... | collective-permute-start | bytes 9224 | tf_op jit(solution)/shard_map/ppermute | solution.py:462
  13.5 12.9 %collective-permute-start.2 = (s32[768]{0:T(1024)S(1)}, s32[768]{0:T(1024)S(1)}, u32[]{:S(2)}, u32[]{:S(2)}) collective-permute-start(s32[768]{0:T(1024)S(1)} %compare_select_fusion), channel_id=1, source_target_pairs={{0,8},{4,12},{8,16},{12,20},{16,24},{20,28},{1,9},{5,13},{9,17},{1... | collective-permute-start | bytes 9224 | tf_op jit(solution)/shard_map/ppermute | solution.py:462
  17.0 13.7 %collective-permute-start.9 = (s32[768]{0:T(1024)}, s32[768]{0:T(1024)S(1)}, u32[]{:S(2)}, u32[]{:S(2)}) collective-permute-start(s32[768]{0:T(1024)} %param.30), channel_id=1, source_target_pairs={{8,0},{12,4},{16,8},{20,12},{24,16},{28,20},{9,1},{13,5},{17,9},{2... | collective-permute-start | bytes 9224 | tf_op jit(solution)/shard_map/ppermute | solution.py:462
  18.3 12.4 %collective-permute-start.8 = (s32[768]{0:T(1024)}, s32[768]{0:T(1024)S(1)}, u32[]{:S(2)}, u32[]{:S(2)}) collective-permute-start(s32[768]{0:T(1024)} %param.30), channel_id=1, source_target_pairs={{4,0},{8,4},{12,8},{16,12},{20,16},{24,20},{28,24},{5,1},{9,5},{13... | collective-permute-start | bytes 9224 | tf_op jit(solution)/shard_map/ppermute | solution.py:462
  19.6 311.4 %all-reduce.3.cloned.1.call-start = ((), (), s32[]{:S(2)}) async-start(), calls=%async_computation.4 | async-start | bytes 6291456 | tf_op jit(solution)/shard_map/psum | solution.py:679
  26.4 12.5 %copy-start.30 = (f32[1024]{0:T(1024)S(1)}, f32[1024]{0:T(1024)}, u32[]{:S(2)}) copy-start(f32[1024]{0:T(1024)} %param.21) | copy-start | bytes 12292
  26.5 12.5 %copy-start.32 = (f32[1024]{0:T(1024)S(1)}, f32[1024]{0:T(1024)}, u32[]{:S(2)}) copy-start(f32[1024]{0:T(1024)} %param.22) | copy-start | bytes 12292
  49.8 40.5 %collective-permute-start.5 = (bf16[768,256]{0,1:T(8,128)(2,1)}, bf16[768,256]{0,1:T(8,128)(2,1)}, u32[]{:S(2)}, u32[]{:S(2)}) collective-permute-start(bf16[768,256]{0,1:T(8,128)(2,1)} %bitcast.13), channel_id=1, source_target_pairs={{0,4},{4,8},{8,12},{12,16},{16,20},{20,24},{24,28},{1,5},{5,9},{9,... | collective-permute-start | bytes 1179656 | tf_op jit(solution)/shard_map/ppermute | solution.py:462
  55.1 36.5 %collective-permute-start.4 = (bf16[768,256]{0,1:T(8,128)(2,1)}, bf16[768,256]{0,1:T(8,128)(2,1)}, u32[]{:S(2)}, u32[]{:S(2)}) collective-permute-start(bf16[768,256]{0,1:T(8,128)(2,1)} %bitcast.13), channel_id=1, source_target_pairs={{0,8},{4,12},{8,16},{12,20},{16,24},{20,28},{1,9},{5,13},{9,17},{1... | collective-permute-start | bytes 1179656 | tf_op jit(solution)/shard_map/ppermute | solution.py:462
  63.6 58.5 %collective-permute-start.1 = (bf16[768,256]{0,1:T(8,128)(2,1)}, bf16[768,256]{0,1:T(8,128)(2,1)}, u32[]{:S(2)}, u32[]{:S(2)}) collective-permute-start(bf16[768,256]{0,1:T(8,128)(2,1)} %bitcast.4), channel_id=1, source_target_pairs={{0,4},{4,8},{8,12},{12,16},{16,20},{20,24},{24,28},{1,5},{5,9},{9,... | collective-permute-start | bytes 1179656 | tf_op jit(solution)/shard_map/ppermute | solution.py:462
  68.7 53.4 %collective-permute-start = (bf16[768,256]{0,1:T(8,128)(2,1)}, bf16[768,256]{0,1:T(8,128)(2,1)}, u32[]{:S(2)}, u32[]{:S(2)}) collective-permute-start(bf16[768,256]{0,1:T(8,128)(2,1)} %bitcast.4), channel_id=1, source_target_pairs={{0,8},{4,12},{8,16},{12,20},{16,24},{20,28},{1,9},{5,13},{9,17},{1... | collective-permute-start | bytes 1179656 | tf_op jit(solution)/shard_map/ppermute | solution.py:462
  73.2 86.9 %collective-permute-start.7 = (bf16[768,256]{0,1:T(8,128)(2,1)S(1)}, bf16[768,256]{0,1:T(8,128)(2,1)}, u32[]{:S(2)}, u32[]{:S(2)}) collective-permute-start(bf16[768,256]{0,1:T(8,128)(2,1)S(1)} %bitcast.134), channel_id=1, source_target_pairs={{8,0},{12,4},{16,8},{20,12},{24,16},{28,20},{9,1},{13,5},{17,9},{2... | collective-permute-start | bytes 1179656 | tf_op jit(solution)/shard_map/ppermute | solution.py:462
  90.3 80.9 %collective-permute-start.6 = (bf16[768,256]{0,1:T(8,128)(2,1)S(1)}, bf16[768,256]{0,1:T(8,128)(2,1)}, u32[]{:S(2)}, u32[]{:S(2)}) collective-permute-start(bf16[768,256]{0,1:T(8,128)(2,1)S(1)} %bitcast.135), channel_id=1, source_target_pairs={{4,0},{8,4},{12,8},{16,12},{20,16},{24,20},{28,24},{5,1},{9,5},{13... | collective-permute-start | bytes 1179656 | tf_op jit(solution)/shard_map/ppermute | solution.py:462
  105.4 15.0 %copy-start.5 = (bf16[768,1024]{1,0:T(8,128)(2,1)S(1)}, bf16[768,1024]{1,0:T(8,128)(2,1)}, u32[]{:S(2)}) copy-start(bf16[768,1024]{1,0:T(8,128)(2,1)} %all-gather.5.cloned.1.call-done) | copy-start | bytes 4718596
  105.4 15.0 %copy-start.9 = (bf16[256,1024]{1,0:T(8,128)(2,1)S(1)}, bf16[256,1024]{1,0:T(8,128)(2,1)}, u32[]{:S(2)}) copy-start(bf16[256,1024]{1,0:T(8,128)(2,1)} %param.24) | copy-start | bytes 1572868
  138.4 47.8 %collective-permute-start.15 = (f32[768,4]{0,1:T(4,128)S(1)}, f32[768,4]{0,1:T(4,128)}, u32[]{:S(2)}, u32[]{:S(2)}) collective-permute-start(f32[768,4]{0,1:T(4,128)S(1)} %bitcast_divide_fusion.2), channel_id=1, source_target_pairs={{8,0},{12,4},{16,8},{20,12},{24,16},{28,20},{9,1},{13,5},{17,9},{2... | collective-permute-start | bytes 36872 | tf_op jit(solution)/shard_map/ppermute | solution.py:462
  139.6 47.8 %collective-permute-start.14 = (f32[768,4]{0,1:T(4,128)S(1)}, f32[768,4]{0,1:T(4,128)}, u32[]{:S(2)}, u32[]{:S(2)}) collective-permute-start(f32[768,4]{0,1:T(4,128)S(1)} %bitcast_divide_fusion.2), channel_id=1, source_target_pairs={{4,0},{8,4},{12,8},{16,12},{20,16},{24,20},{28,24},{5,1},{9,5},{13... | collective-permute-start | bytes 36872 | tf_op jit(solution)/shard_map/ppermute | solution.py:462
  140.9 47.3 %collective-permute-start.11 = (f32[768,4]{0,1:T(4,128)S(1)}, f32[768,4]{0,1:T(4,128)}, u32[]{:S(2)}, u32[]{:S(2)}) collective-permute-start(f32[768,4]{0,1:T(4,128)S(1)} %get-tuple-element.101), channel_id=1, source_target_pairs={{8,0},{12,4},{16,8},{20,12},{24,16},{28,20},{9,1},{13,5},{17,9},{2... | collective-permute-start | bytes 36872 | tf_op jit(solution)/shard_map/ppermute | solution.py:462
  160.1 28.1 %collective-permute-start.10 = (f32[768,4]{0,1:T(4,128)S(1)}, f32[768,4]{0,1:T(4,128)S(1)}, u32[]{:S(2)}, u32[]{:S(2)}) collective-permute-start(f32[768,4]{0,1:T(4,128)S(1)} %get-tuple-element.101), channel_id=1, source_target_pairs={{4,0},{8,4},{12,8},{16,12},{20,16},{24,20},{28,24},{5,1},{9,5},{13... | collective-permute-start | bytes 36872 | tf_op jit(solution)/shard_map/ppermute | solution.py:462
  183.9 18.2 %collective-permute-start.13 = (bf16[768,256]{0,1:T(8,128)(2,1)}, bf16[768,256]{0,1:T(8,128)(2,1)}, u32[]{:S(2)}, u32[]{:S(2)}) collective-permute-start(bf16[768,256]{0,1:T(8,128)(2,1)} %get-tuple-element.109), channel_id=1, source_target_pairs={{8,0},{12,4},{16,8},{20,12},{24,16},{28,20},{9,1},{13,5},{17,9},{2... | collective-permute-start | bytes 1179656 | tf_op jit(solution)/shard_map/ppermute | solution.py:462
  186.2 16.0 %collective-permute-start.12 = (bf16[768,256]{0,1:T(8,128)(2,1)}, bf16[768,256]{0,1:T(8,128)(2,1)}, u32[]{:S(2)}, u32[]{:S(2)}) collective-permute-start(bf16[768,256]{0,1:T(8,128)(2,1)} %get-tuple-element.109), channel_id=1, source_target_pairs={{4,0},{8,4},{12,8},{16,12},{20,16},{24,20},{28,24},{5,1},{9,5},{13... | collective-permute-start | bytes 1179656 | tf_op jit(solution)/shard_map/ppermute | solution.py:462
  189.0 32.2 %copy-start.29 = (f32[4,2304]{1,0:T(4,128)}, f32[4,2304]{1,0:T(4,128)S(1)}, u32[]{:S(2)}) copy-start(f32[4,2304]{1,0:T(4,128)S(1)} %maximum_bitcast_fusion) | copy-start | bytes 110596
  222.8 14.0 %slice-start = ((f32[768,4,64]{0,2,1:T(8,128)}), f32[768,4,32]{0,2,1:T(8,128)S(1)}, s32[]{:S(2)}) async-start(f32[768,4,64]{0,2,1:T(8,128)} %fusion.35), calls=%async_computation.5 | async-start | bytes 786432 | tf_op jit(solution)/shard_map/slice | solution.py:474
  222.8 15.0 %copy-start.14 = (f32[768,4,16,2]{0,3,2,1:T(2,128)S(1)}, f32[768,4,16,2]{0,3,2,1:T(2,128)}, u32[]{:S(2)}) copy-start(f32[768,4,16,2]{0,3,2,1:T(2,128)} %reshape.608) | copy-start | bytes 1179652
  256.0 282.6 %reduce-scatter.2.cloned.1.call-start = ((), (), s32[]{:S(2)}) async-start(), calls=%async_computation.2 | async-start | bytes 3932160 | tf_op jit(solution)/shard_map/reduce_scatter | solution.py:561
  274.5 56.5 %copy-start.24 = (f32[768]{0:T(1024)S(1)}, f32[768]{0:T(1024)}, u32[]{:S(2)}) copy-start(f32[768]{0:T(1024)} %copy-done.23) | copy-start | bytes 9220
  274.5 56.5 %copy-start.26 = (f32[768]{0:T(1024)S(1)}, f32[768]{0:T(1024)}, u32[]{:S(2)}) copy-start(f32[768]{0:T(1024)} %copy-done.25) | copy-start | bytes 9220
  274.5 56.5 %copy-start.31 = (f32[1024]{0:T(1024)S(1)}, f32[1024]{0:T(1024)}, u32[]{:S(2)}) copy-start(f32[1024]{0:T(1024)} %param.21) | copy-start | bytes 12292
  276.5 60.2 %copy-start.15 = (bf16[768,256]{1,0:T(8,128)(2,1)S(1)}, bf16[768,256]{1,0:T(8,128)(2,1)}, u32[]{:S(2)}) copy-start(bf16[768,256]{1,0:T(8,128)(2,1)} %param.29) | copy-start | bytes 1179652
  (29 other events, 113.9 us)
Sparse Core Ops, SparseCore 0:
  9.6 22.5 all-gather.2
  33.7 19.8 all-gather.4
  256.1 74.8 all-reduce.2
  333.4 38.0 reduce-scatter.1
